TPU v7x, 128 devices: a whole 4x4x4 slice. The times are simulated.
128 devices in a mesh: grp: 4 (over z_hi, core), leaf: 32 (over z_lo, y, x).
Axes of the slice: x: 4, y: 4, z: 4 (z_hi: 2, z_lo: 2; z = z_hi * 2 + z_lo), core: 2. Of those that a mesh axis runs over, the one named last changes fastest.
Arguments:
- features: float32 [131072, 128], P(('grp', 'leaf')), may hold values from -6 to 6
- tree_order: int32 [128, 1024], P(('grp', 'leaf')), may hold values from 0 to 1023, each once within a row
- gain_leaf: float32 [128], replicated, may hold values from 0.1 to 1.9
- w_qkv_leaf: float32 [128, 384], replicated
- w_out_leaf: float32 [128, 128], replicated, may hold values from -0.5 to 0.5
- w_pool1: float32 [512, 256], replicated, may hold values from -0.5 to 0.5
- w_pool2: float32 [1024, 384], replicated, may hold values from -0.375 to 0.375
- w_pool3: float32 [1536, 512], replicated, may hold values from -0.21875 to 0.21875
- gain_coarse: float32 [512], replicated, may hold values from 0.1 to 1.9
- w_query: float32 [512, 512], replicated
- w_keyval: float32 [512, 1024], replicated
- w_out: float32 [512, 512], replicated, may hold values from -0.25 to 0.25
- cotangent: float32 [2048, 512], P(('grp', 'leaf')), may hold values from -6 to 6
Outputs:
- output: float32 [2048, 512], P(('grp', 'leaf'))
- grad_gain_leaf: float32 [128], replicated
- grad_qkv_leaf: float32 [128, 384], replicated
- grad_out_leaf: float32 [128, 128], replicated
- grad_pool1: float32 [512, 256], replicated
- grad_pool2: float32 [1024, 384], replicated
- grad_pool3: float32 [1536, 512], replicated
- grad_gain_coarse: float32 [512], replicated
- grad_query: float32 [512, 512], replicated
- grad_keyval: float32 [512, 1024], replicated
- grad_out: float32 [512, 512], replicated
Inputs may be any that keep to these rules, and one draw needn't show every extreme that they name: `tree_order`: each row lists the 1024 particles of one device, each once.
All inputs are finite; a program needn't handle non-finite values.
Results may differ from a plain program's by a relative error of at most 0.0003.
Values sent between devices are 32-bit elements; how exact they have to be, the bound alone decides.
No kernel may reach another device: no remote copies, remote signals or barrier semaphores. Data moves between devices by JAX's collectives and lax.ppermute only.
A program may use at most 128 MiB of HBM per device.

v0:
```python
import jax
import jax.numpy as jnp
from jax import lax
from jax.experimental import pallas as pl
from jax.experimental.pallas import tpu as pltpu
from jax.sharding import Mesh
from jax.sharding import PartitionSpec as P

GRP = ("zh", "co")
LEAF = ("zl", "y", "x")
ALL = GRP + LEAF
CHIPS = ("zh",) + LEAF
N_LEAF = 32
HEADS = 16
SCALE = 32 ** (-0.5)
F32 = jnp.float32


def split(value):
    high = value.astype(jnp.bfloat16)
    return high, (value - high.astype(F32)).astype(jnp.bfloat16)


def dot3(left, right, dims):
    left_high, left_low = split(left)
    right_high, right_low = split(right)
    go = lambda a, b: lax.dot_general(a, b, (dims, ((), ())), preferred_element_type=F32)
    return go(left_high, right_high) + (go(left_high, right_low) + go(left_low, right_high))


def mm(left, right):
    return dot3(left, right, ((1,), (0,)))


def mm_t(left, right):
    return dot3(left, right, ((1,), (1,)))


def t_mm(left, right):
    return dot3(left, right, ((0,), (0,)))


def full(left, right, dims):
    return lax.dot_general(
        left, right, (dims, ((), ())), precision=lax.Precision.HIGHEST, preferred_element_type=F32
    )


def mm6(left, right):
    return full(left, right, ((1,), (0,)))


def mm6_t(left, right):
    return full(left, right, ((1,), (1,)))


def t_mm6(left, right):
    return full(left, right, ((0,), (0,)))


def lanes(at):
    lane = lax.broadcasted_iota(jnp.int32, (1, 128), 1)
    return ((lane >= 32 * at) & (lane < 32 * at + 32)).astype(F32)


def turn(value, by):
    by = by % 128
    return value if by == 0 else pltpu.roll(value, by, 1)


def inverse_rms(values):
    return lax.rsqrt(jnp.mean(values * values, axis=-1, keepdims=True) + 1e-06)


def sigmoid(pre):
    return 1.0 / (1.0 + jnp.exp(-pre))


def softmax(scores):
    weights = jnp.exp(scores - jnp.max(scores, axis=-1, keepdims=True))
    return weights / jnp.sum(weights, axis=-1, keepdims=True)


def four(value):
    return jnp.concatenate([value * lanes(h) for h in range(4)], axis=0)


def slot_one(rows, at):
    return rows.reshape(8, 4, 32, rows.shape[-1])[:, at].reshape(256, rows.shape[-1])


def slot_two(rows, at):
    return rows.reshape(8, 4, 8, rows.shape[-1])[:, at].reshape(64, rows.shape[-1])


def stride_get(ref, at, stride):
    blocks = [ref[j, pl.ds(at, 8, stride=stride), :] for j in range(ref.shape[0])]
    return jnp.concatenate(blocks, axis=1)


def stride_put(ref, at, stride, value):
    for j in range(ref.shape[0]):
        ref[j, pl.ds(at, 8, stride=stride), :] = value[:, 128 * j : 128 * j + 128]


def put_blocks(ref, value):
    for j in range(ref.shape[0]):
        ref[j] = value[:, 128 * j : 128 * j + 128]


def get_blocks(ref):
    return jnp.concatenate([ref[j] for j in range(ref.shape[0])], axis=1)


def slot_three(ref, at):
    return jnp.concatenate([stride_get(ref, 2 * at + a, 8) for a in range(2)], axis=0)


def forward_kernel(
    order, features, gain_leaf, w_qkv, w_out_leaf, gain_coarse, cotangent,
    far_one, far_two, far_three, far_query, far_keyval, far_out,
    unit, packed, weights, attended, mixed, pre_one, pre_two, two, coarse, rows, message, roots,
    ordered, natural, w_one, w_two, w_three, w_query, w_keyval, w_out, arrived,
):
    pairs = (
        (far_one, w_one), (far_two, w_two), (far_three, w_three),
        (far_query, w_query), (far_keyval, w_keyval), (far_out, w_out),
    )
    copies = [pltpu.make_async_copy(*pair, arrived.at[i]) for i, pair in enumerate(pairs)]
    for copy in copies:
        copy.start()
    wait = lambda i: copies[i].wait()

    def fetch(step, carry):
        ball, rest = step // 16, step % 16
        base = ball * 128 + (rest % 4) * 4 + rest // 4
        for d2 in range(4):
            for a in range(2):
                source = order[0, base + 64 * a + 16 * d2]
                ordered[pl.ds(step * 8 + 2 * d2 + a, 1), :] = features[pl.ds(source, 1), :]
        return carry

    lax.fori_loop(0, 128, fetch, 0, unroll=8)
    unit[...] = ordered[...] * inverse_rms(ordered[...])
    packed[...] = mm6(unit[...] * gain_leaf[...], w_qkv[...])

    def ball(step, carry):
        at = pl.ds(step * 128, 128)
        values = packed[at, 256:]
        scores = mm_t(four(packed[at, :128] * SCALE), packed[at, 128:256])
        probs = softmax(scores)
        weights[pl.ds(step * 512, 512), :] = probs
        wide = jnp.concatenate([probs[128 * h : 128 * h + 128] for h in range(4)], axis=1)
        attended[at, :] = mm(wide, four(values))
        return carry

    lax.fori_loop(0, 8, ball, 0, unroll=8)
    joined = ordered[...] + mm6(attended[...], w_out_leaf[...])
    mixed[...] = joined
    wait(0)
    pre = mm6(jnp.concatenate([slot_one(joined, d) for d in range(4)], axis=1), w_one[...])
    pre_one[...] = pre
    one = pre * sigmoid(pre)
    wait(1)
    pre = mm6(jnp.concatenate([slot_two(one, d) for d in range(4)], axis=1), w_two[...])
    pre_two[...] = pre
    put_blocks(two, pre * sigmoid(pre))
    wait(2)
    top = mm6(jnp.concatenate([slot_three(two, d) for d in range(4)], axis=1), w_three[...])
    for a in range(2):
        stride_put(natural, a, 2, top[8 * a : 8 * a + 8])
    top = get_blocks(natural)
    coarse[...] = top
    means = jnp.concatenate(
        [jnp.mean(top[8 * r : 8 * r + 8], axis=0, keepdims=True) for r in range(2)]
        + [jnp.zeros((6, 512), F32)],
        axis=0,
    )
    normed = jnp.concatenate([top * inverse_rms(top), means * inverse_rms(means)], axis=0)
    normed = normed * gain_coarse[...]
    rows[...] = normed
    for i in range(3, 6):
        wait(i)
    queries = mm6(normed[:16], w_query[...])
    keyval = mm6(normed, w_keyval[...])
    d_bottleneck = mm6_t(cotangent[...], w_out[...])
    parts = (queries, keyval[:16, :512], keyval[:16, 512:], d_bottleneck)
    for h in range(HEADS):
        block = slice(128 * (h // 4), 128 * (h // 4) + 128)
        message[h] = sum(
            turn(part[:, block], 32 * (c - h % 4)) * lanes(c) for c, part in enumerate(parts)
        )
    for j in range(8):
        roots[2 * j : 2 * j + 2, :] = keyval[16:18, 128 * j : 128 * j + 128]
    for j in range(4):
        roots[16 + 2 * j : 18 + 2 * j, :] = normed[16:18, 128 * j : 128 * j + 128]


def message_kernel(group, main, roots, one, two, three, message, root_rows, sorted_roots):
    for k, part in enumerate((roots, one, two, three)):
        sorted_roots[group[0] ^ k] = part[...]
    roots = sorted_roots
    block = lambda j: roots[:, 2 * j : 2 * j + 2, :].reshape(8, 128)
    for h in range(HEADS):
        side = turn(block(h // 4), -32 * (h % 4)) * lanes(0)
        side = side + turn(block(4 + h // 4), 32 - 32 * (h % 4)) * lanes(1)
        for half in range(2):
            message[2 * h + half, :16, :] = main[h]
            message[2 * h + half, 16:, :] = side
    for j in range(4):
        root_rows[:, 128 * j : 128 * j + 128] = block(8 + j)


def attend_kernel(half, got, message):
    at = pl.multiple_of(half[0] * 8, 8)
    mine = got[:, pl.ds(at, 8), :].reshape(256, 128)
    every = got[:, :16, :].reshape(512, 128)
    away = got[:, 16:, :].reshape(256, 128)
    queries = mine * lanes(0) * SCALE
    d_out = mine * lanes(3)

    def scores_of(keys, values):
        probs = softmax(mm6_t(queries, keys))
        d_probs = mm6_t(d_out, values)
        d_scores = probs * (d_probs - jnp.sum(probs * d_probs, axis=-1, keepdims=True))
        return probs, d_scores * SCALE

    probs, d_scores = scores_of(turn(every, -32), turn(every, 32))
    front = mm(probs, turn(every, -64) * lanes(0)) + mm(d_scores, every * lanes(1))
    back = t_mm(d_scores, turn(mine, 64) * lanes(2)) + t_mm(probs, d_out)
    probs, d_scores = scores_of(away, turn(away, 64))
    front = front + mm(probs, turn(away, -32) * lanes(0))
    front = front + mm(d_scores, turn(away, 32) * lanes(1))
    side = t_mm(d_scores, mine * lanes(0)) + t_mm(probs, turn(mine, 64) * lanes(1))
    message[:, :16, :] = back.reshape(N_LEAF, 16, 128)
    message[:, pl.ds(at, 8), :] = message[:, pl.ds(at, 8), :] + front.reshape(N_LEAF, 8, 128)
    message[:, 16:, :] = side.reshape(N_LEAF, 8, 128)


def unpack_kernel(got, rows, root_rows, cotangent, bottleneck, d_queries, d_keyval, d_roots, pack):
    pack[16:, :1024] = jnp.zeros((8, 1024), F32)
    pack[16:, 2560:] = jnp.zeros((8, 512), F32)
    pack[:16, 2048:2560] = rows[:16, :]
    pack[16:, 2048:2560] = root_rows[...]
    pack[:16, 2560:] = cotangent[...]
    for block in range(4):
        heads = [got[2 * h] + got[2 * h + 1] for h in range(4 * block, 4 * block + 4)]
        pick = lambda c, rows: sum(
            turn(heads[k][rows], 32 * (k - c)) * lanes(k) for k in range(4)
        )
        own, far = slice(0, 16), slice(16, 24)
        for c, ref in enumerate((bottleneck, d_queries, d_keyval, d_keyval)):
            at = 128 * block + (512 if c == 3 else 0)
            value = pick(c, own)
            ref[:, at : at + 128] = value
            pack[:16, 512 * c + 128 * block : 512 * c + 128 * block + 128] = value
        for c in range(2):
            value = pick(c, far)
            at = 8 * c + 2 * block
            d_roots[:, at : at + 2, :] = value.reshape(4, 2, 128)
            at = 1024 + 512 * c + 128 * block
            pack[16:, at : at + 128] = value


def upper_kernel(core, mine, other, grads):
    both = lambda at, width: jnp.concatenate(
        [mine[:, pl.ds(at, width)], other[:, pl.ds(at, width)]], axis=0
    )
    half = lambda at, width: both(pl.multiple_of(at + core[0] * width, 128), width)
    normed = both(2048, 512)
    grads[:, :256] = t_mm(both(0, 512), half(2560, 256))
    grads[:, 256:512] = t_mm(normed, half(512, 256))
    grads[:, 512:] = t_mm(normed, half(1024, 512))


def assemble_upper_kernel(core, mine, other, grad_query, grad_keyval, grad_out):
    def fill(half, source):
        grad_out[:, 256 * half : 256 * half + 256] = source[:, :256]
        grad_query[:, 256 * half : 256 * half + 256] = source[:, 256:512]
        grad_keyval[:, 512 * half : 512 * half + 512] = source[:, 512:]

    for half in range(2):

        @pl.when(core[0] == half)
        def _():
            fill(half, mine)
            fill(1 - half, other)


def rms_backward(d_normed, values, gain):
    scale = inverse_rms(values)
    unit = values * scale
    d_unit = d_normed * gain
    d_values = scale * (d_unit - unit * jnp.mean(d_unit * unit, axis=-1, keepdims=True))
    return d_values, jnp.sum(d_normed * unit, axis=0, keepdims=True)


def backward_kernel(
    group, d_roots, roots_one, roots_two, roots_three, bottleneck, w_out, d_queries, d_keyval, rows, coarse, cotangent, gain_coarse, w_query, w_keyval,
    w_three, w_two, w_one, w_out_leaf, w_qkv, gain_leaf,
    unit, packed, weights, attended, mixed, pre_one, pre_two, two,
    output, keep, send,
    d_coarse, d_two, d_packed, d_attended,
):
    def put(half, chips, at, value):
        chips, at = pl.ds(*chips), pl.ds(*at)

        @pl.when(core == half)
        def _():
            keep[chips, at, :] = value

        @pl.when(core != half)
        def _():
            send[chips, at, :] = value

    core = group[0] % 2
    output[...] = coarse[...] + mm6(bottleneck[...], w_out[...])
    far = sum(ref[group[0]] for ref in (d_roots, roots_one, roots_two, roots_three))
    far = jnp.concatenate([far[2 * j : 2 * j + 2] for j in range(8)], axis=1)
    d_kv = jnp.concatenate([d_keyval[...], far, jnp.zeros((6, 1024), F32)], axis=0)
    d_rows = mm6_t(d_kv, w_keyval[...])
    top = coarse[...]
    d_top, gain_a = rms_backward(
        d_rows[:16] + mm6_t(d_queries[...], w_query[...]), top, gain_coarse[...]
    )
    means = jnp.concatenate(
        [jnp.mean(top[8 * r : 8 * r + 8], axis=0, keepdims=True) for r in range(2)], axis=0
    )
    d_means, gain_b = rms_backward(d_rows[16:18], means, gain_coarse[...])
    d_means = d_means * 0.125
    d_means = jnp.concatenate(
        [jnp.broadcast_to(d_means[r : r + 1], (8, 512)) for r in range(2)], axis=0
    )
    put_blocks(d_coarse, cotangent[...] + d_top + d_means)
    gain_c = gain_a + gain_b

    d_top = jnp.concatenate([stride_get(d_coarse, a, 2) for a in range(2)], axis=0)
    for d in range(4):
        at = slice(384 * d, 384 * d + 384)
        grad = t_mm(slot_three(two, d), d_top)
        for i in range(4):
            block = grad[:, 128 * i : 128 * i + 128].reshape(16, 24, 128)
            put(i // 2, (16 * d, 16), (24 * (i % 2), 24), block)
        part = mm6_t(d_top, w_three[at, :])
        for a in range(2):
            stride_put(d_two, 2 * d + a, 8, part[8 * a : 8 * a + 8])
    pre = pre_two[...]
    gate = sigmoid(pre)
    d_pre = get_blocks(d_two) * (gate * (1.0 + pre * (1.0 - gate)))
    pre = pre_one[...]
    gate = sigmoid(pre)
    one = pre * gate
    parts = []
    for d in range(4):
        at = slice(256 * d, 256 * d + 256)
        grad = t_mm(slot_two(one, d), d_pre)
        for i in range(3):
            block = grad[:, 128 * i : 128 * i + 128].reshape(32, 8, 128)
            put(d // 2, (32 * (d % 2), 32), (48 + 8 * i, 8), block)
        parts.append(mm_t(d_pre, w_two[at, :]).reshape(8, 1, 8, 256))
    d_one = jnp.concatenate(parts, axis=1).reshape(256, 256)
    d_pre = d_one * (gate * (1.0 + pre * (1.0 - gate)))
    joined = mixed[...]
    parts = []
    for d in range(4):
        at = slice(128 * d, 128 * d + 128)
        grad = t_mm(slot_one(joined, d), d_pre)
        for i in range(2):
            put(i, (16 * d, 16), (72, 8), grad[:, 128 * i : 128 * i + 128].reshape(16, 8, 128))
        parts.append(mm_t(d_pre, w_one[at, :]).reshape(8, 1, 32, 128))
    d_mixed = jnp.concatenate(parts, axis=1).reshape(1024, 128)
    grad_out_leaf = t_mm(attended[...], d_mixed)
    d_attended[...] = mm_t(d_mixed, w_out_leaf[...])

    def ball(step, carry):
        at = pl.ds(step * 128, 128)
        probs = weights[pl.ds(step * 512, 512), :]
        d_out = four(d_attended[at, :])
        d_probs = mm6_t(d_out, packed[at, 256:])
        d_scores = probs * (d_probs - jnp.sum(probs * d_probs, axis=-1, keepdims=True)) * SCALE
        wide = jnp.concatenate([d_scores[128 * h : 128 * h + 128] for h in range(4)], axis=1)
        d_packed[at, :128] = mm(wide, four(packed[at, 128:256]))
        d_packed[at, 128:256] = t_mm(d_scores, four(packed[at, :128]))
        d_packed[at, 256:] = t_mm(probs, d_out)
        return carry

    lax.fori_loop(0, 8, ball, 0, unroll=4)
    grad_qkv = t_mm(unit[...] * gain_leaf[...], d_packed[...])
    blocks = [grad_qkv[:, 128 * i : 128 * i + 128] for i in range(3)] + [grad_out_leaf]
    for i, block in enumerate(blocks):
        put(i // 2, (16 * (i % 2), 16), (80, 8), block.reshape(16, 8, 128))
    d_normed = mm_t(d_packed[...], w_qkv[...])
    gains = jnp.concatenate(
        [jnp.sum(d_normed * unit[...], axis=0, keepdims=True)]
        + [gain_c[:, 128 * j : 128 * j + 128] for j in range(4)]
        + [jnp.zeros((3, 128), F32)],
        axis=0,
    )
    put(0, (32, 1), (80, 8), gains.reshape(1, 8, 128))
    put(0, (33, 31), (80, 8), jnp.zeros((31, 8, 128), F32))
    put(1, (32, 32), (80, 8), jnp.zeros((32, 8, 128), F32))


def place(half, near, outs, staged, left):
    three, two, one = staged
    homes = (
        outs[0].at[:, pl.ds(pl.multiple_of(half * 256, 128), 256)],
        outs[1].at[pl.ds(pl.multiple_of(half * 512, 8), 512), :],
        outs[2].at[:, pl.ds(pl.multiple_of(half * 128, 128), 128)],
    )
    leaving = []
    for i in range(3):
        if i == 0:
            for j in range(2):
                block = near[:, 24 * j : 24 * j + 24, :]
                three[:, 128 * j : 128 * j + 128] = block.reshape(1536, 128)
        elif i == 1:
            for j in range(3):
                block = near[:, 48 + 8 * j : 56 + 8 * j, :]
                two[:, 128 * j : 128 * j + 128] = block.reshape(512, 128)
        else:
            one[...] = near[:, 72:80, :].reshape(512, 128)
        leaving.append(pltpu.make_async_copy(staged[i], homes[i], left.at[i]))
        leaving[-1].start()
    return leaving


def mine_kernel(core, near, three, two, one, stage_a, stage_b, stage_c, left):
    for copy in place(core[0], near, (three, two, one), (stage_a, stage_b, stage_c), left):
        copy.wait()


def other_kernel(
    core, own, near, three_in, two_in, one_in,
    three, two, one, gain_leaf, gain_coarse, grad_qkv, grad_out_leaf,
    stage_a, stage_b, stage_c, left,
):
    del three_in, two_in, one_in
    stages = (stage_a, stage_b, stage_c)
    leaving = place(1 - core[0], near, (three, two, one), stages, left)

    def fill(half, blocks):
        first, second = blocks[0:16].reshape(128, 128), blocks[16:32].reshape(128, 128)
        if half == 0:
            grad_qkv[:, :128] = first
            grad_qkv[:, 128:256] = second
            gain_leaf[...] = blocks[32, 0, :]
            for i in range(4):
                gain_coarse[128 * i : 128 * i + 128] = blocks[32, 1 + i, :]
        else:
            grad_qkv[:, 256:] = first
            grad_out_leaf[...] = second

    for half in range(2):

        @pl.when(core[0] == half)
        def _():
            fill(half, own[:, 80:88, :])
            fill(1 - half, near[:, 80:88, :])

    for copy in leaving:
        copy.wait()


def assemble(core, mine, other):
    pools = [jax.ShapeDtypeStruct(shape, F32) for shape in ((1536, 512), (1024, 384), (512, 256))]
    small = [
        jax.ShapeDtypeStruct(shape, F32) for shape in ((128,), (512,), (128, 384), (128, 128))
    ]
    smem, vmem, hbm = (
        pl.BlockSpec(memory_space=space) for space in (pltpu.SMEM, pltpu.VMEM, pl.ANY)
    )
    rooms = [pltpu.VMEM(shape, F32) for shape in ((1536, 256), (512, 384), (512, 128))]
    rooms.append(pltpu.SemaphoreType.DMA((3,)))
    params = pltpu.CompilerParams(vmem_limit_bytes=24 * 2**20)
    begun = pl.pallas_call(
        mine_kernel,
        out_shape=pools,
        in_specs=[smem, vmem],
        out_specs=[hbm] * 3,
        scratch_shapes=rooms,
        compiler_params=params,
    )(core, mine)
    return pl.pallas_call(
        other_kernel,
        out_shape=pools + small,
        in_specs=[smem, vmem, vmem] + [hbm] * 3,
        out_specs=[hbm] * 3 + [vmem] * 4,
        scratch_shapes=rooms,
        input_output_aliases={3: 0, 4: 1, 5: 2},
        compiler_params=params,
    )(core, mine, other, *begun)


def call(kernel, outs, scratch=(), smem_first=False, cost=None, far=0, limit=56):
    shapes = [jax.ShapeDtypeStruct(shape, F32) for shape in outs]

    rooms = [pltpu.VMEM(shape, F32) for shape in scratch]

    def run(*args):
        specs = [pl.BlockSpec(memory_space=pltpu.VMEM)] * len(args)
        if smem_first:
            specs[0] = pl.BlockSpec(memory_space=pltpu.SMEM)
        if far:
            specs[-far:] = [pl.BlockSpec(memory_space=pl.ANY)] * far
            rooms.append(pltpu.SemaphoreType.DMA((far,)))
        return pl.pallas_call(
            kernel,
            out_shape=shapes,
            in_specs=specs,
            out_specs=[pl.BlockSpec(memory_space=pltpu.VMEM)] * len(shapes),
            scratch_shapes=rooms,
            cost_estimate=cost,
            compiler_params=pltpu.CompilerParams(vmem_limit_bytes=limit * 2**20),
        )(*args)

    return run


def group_swaps(value):
    return [lax.ppermute(value, GRP, [(i, i ^ k) for i in range(4)]) for k in range(1, 4)]


def spread(value, axes, parts):
    wide = jnp.broadcast_to(value[None], (parts,) + value.shape)
    return lax.all_to_all(wide, axes, 0, 0, tiled=True)


def shards(
    features, tree_order, gain_leaf, w_qkv, w_out_leaf, w_one, w_two, w_three, gain_coarse,
    w_query, w_keyval, w_out, cotangent,
):
    half = (lax.axis_index("x") % 2).astype(jnp.int32).reshape(1)
    group = lax.axis_index(GRP).astype(jnp.int32).reshape(1)
    core = lax.axis_index("co").astype(jnp.int32).reshape(1)
    gain_leaf = gain_leaf.reshape(1, 128)
    gain_coarse = gain_coarse.reshape(1, 512)
    saved_shapes = [
        (1024, 128), (1024, 384), (4096, 128), (1024, 128), (1024, 128), (256, 256), (64, 384),
        (3, 64, 128),
    ]
    *saved, coarse, rows, main, roots = call(
        forward_kernel,
        saved_shapes + [(16, 512), (24, 512), (HEADS, 16, 128), (24, 128)],
        [(1024, 128), (4, 16, 128), (512, 256), (1024, 384), (1536, 512), (512, 512), (512, 1024),
         (512, 512)],
        True,
        far=6,
    )(
        tree_order, features, gain_leaf, w_qkv, w_out_leaf, gain_coarse, cotangent,
        w_one, w_two, w_three, w_query, w_keyval, w_out,
    )
    message, root_rows = call(
        message_kernel, [(N_LEAF, 24, 128), (8, 512)], [(4, 24, 128)], True, limit=16
    )(group, main, roots, *group_swaps(roots))
    got = lax.all_to_all(message, LEAF, 0, 0, tiled=True)
    message = call(attend_kernel, [(N_LEAF, 24, 128)], (), True, limit=16)(half, got)[0]
    got = lax.all_to_all(message, LEAF, 0, 0, tiled=True)
    bottleneck, d_queries, d_keyval, d_roots, pack = call(
        unpack_kernel, [(16, 512), (16, 512), (16, 1024), (4, 16, 128), (24, 3072)]
    )(got, rows, root_rows, cotangent)
    swap = lambda v: lax.ppermute(v, "co", [(0, 1), (1, 0)])
    upper = call(upper_kernel, [(512, 1024)], (), True, limit=16)(core, pack, swap(pack))[0]
    upper, *far = lax.optimization_barrier((upper, *group_swaps(d_roots)))
    upper = lax.all_to_all(upper.reshape(64, 8, 1024), CHIPS, 0, 0, tiled=True)
    output, keep, send = call(
        backward_kernel,
        [(16, 512), (64, 88, 128), (64, 88, 128)],
        [(4, 16, 128), (3, 64, 128), (1024, 384), (1024, 128)],
        True,
        pl.CostEstimate(flops=12_000_000_000, bytes_accessed=20_000_000, transcendentals=0),
    )(
        group, d_roots, *far, bottleneck, w_out, d_queries, d_keyval, rows, coarse, cotangent,
        gain_coarse, w_query, w_keyval, w_three, w_two, w_one, w_out_leaf, w_qkv, gain_leaf,
        *saved,
    )
    send, upper = lax.optimization_barrier((send, upper))
    upper = spread(jnp.sum(upper, axis=0), CHIPS, 64).reshape(512, 1024)
    late, upper = lax.optimization_barrier((keep + swap(send), upper))
    late = jnp.sum(lax.all_to_all(late, CHIPS, 0, 0, tiled=True), axis=0)
    late = spread(late, CHIPS, 64)
    upper = call(assemble_upper_kernel, [(512, 512), (512, 1024), (512, 512)], (), True)(
        core, upper, swap(upper)
    )
    late, *upper = lax.optimization_barrier((late, *upper))
    three, two, one, gain_leaf, gain_coarse, grad_qkv, grad_out_leaf = assemble(
        core, late, swap(late)
    )
    return (
        output, gain_leaf, grad_qkv, grad_out_leaf, one, two, three, gain_coarse, *upper,
    )


def solution(mesh):
    fine = Mesh(mesh.devices.reshape(2, 2, 2, 4, 4), ALL)
    cut = P(ALL, None)
    return jax.shard_map(
        shards,
        mesh=fine,
        in_specs=(cut, cut) + (P(),) * 10 + (cut,),
        out_specs=(cut,) + (P(),) * 10,
        check_vma=False,
    )
```

profile of v0, /device:TPU:1, one launch (start us, length us, event | category | flops | bytes accessed | tf_op | source)
XLA Modules:
  0.0 261.3 jit_solution(1861201784747593915)
XLA Ops:
  0.6 15.2 %shard_map.212 = (f32[1024,128]{1,0:T(8,128)}, f32[1024,384]{1,0:T(8,128)}, f32[4096,128]{1,0:T(8,128)}, f32[1024,128]{1,0:T(8,128)}, f32[1024,128]{1,0:T(8,128)...) custom-call(s32[1,1024]{1,0:T(1,128)} %order.1, ...), custom_call_target="tpu_custom_call" | custom-call | tf_op jit(solution)/shard_map/pallas_call | solution.py:507
  15.9 5.1 %collective-permute-start.2 = (f32[24,128]{1,0:T(8,128)}, f32[24,128]{1,0:T(8,128)S(1)}, u32[]{:S(2)}, u32[]{:S(2)}) collective-permute-start(f32[24,128]{1,0:T(8,128)} %get-tuple-element.59.roots), channel_id=1, source_target_pairs={{0,96},{32,64},{64,32},{96,0},{1,97},{33,65},{65,33},{97,1},{2,98}... | collective-permute-start | bytes 36872 | tf_op jit(solution)/shard_map/ppermute | solution.py:521
  20.9 0.0 collective-permute-start.1
  20.9 0.5 collective-permute-start
  21.4 1.1 collective-permute-done.2.three
  22.5 2.7 %collective-permute-done.1.two = f32[24,128]{1,0:T(8,128)S(1)} collective-permute-done((f32[24,128]{1,0:T(8,128)}, f32[24,128]{1,0:T(8,128)S(1)}, u32[]{:S(2)}, u32[]{:S(2)}) %collective-permute-start.1) | collective-permute-done | bytes 12320 | tf_op jit(solution)/shard_map/ppermute | solution.py:521
  25.2 0.9 copy-done.1
  26.1 0.7 copy-done.3
  26.8 0.9 shard_map.213
  27.7 0.6 copy-done.2
  28.3 7.8 %all-to-all-start = ((f32[32,24,128]{2,1,0:T(8,128)}), f32[32,24,128]{2,1,0:T(8,128)S(1)}, u32[]{:S(2)}, u32[]{:S(2)}) async-start(f32[32,24,128]{2,1,0:T(8,128)} %get-tuple-element.60), calls=%async_computation | async-start | bytes 786432 | tf_op jit(solution)/shard_map/all_to_all | solution.py:556
  36.0 8.3 %all-to-all-done.got = f32[32,24,128]{2,1,0:T(8,128)S(1)} async-done(((f32[32,24,128]{2,1,0:T(8,128)}), f32[32,24,128]{2,1,0:T(8,128)S(1)}, u32[]{:S(2)}, u32[]{:S(2)}) %all-to-all-start) | async-done | bytes 393248 | tf_op jit(solution)/shard_map/all_to_all | solution.py:556
  44.3 2.9 %shard_map.214 = f32[32,24,128]{2,1,0:T(8,128)S(1)} custom-call(s32[1]{0:T(128)} %bitcast.1.half, f32[32,24,128]{2,1,0:T(8,128)S(1)} %all-to-all-done.got), custom_call_target="tpu_custom_call" | custom-call | tf_op jit(solution)/shard_map/pallas_call | solution.py:507
  47.2 12.6 %all_to_all.30.got = f32[32,24,128]{2,1,0:T(8,128)} all-to-all(f32[32,24,128]{2,1,0:T(8,128)S(1)} %shard_map.214), channel_id=1, replica_groups=mesh['zh'=2,'co'=2,'zl'=2,'y'=4,'x'=4] {'zl','y','x'}, dimensions={0} | all-to-all | bytes 786432 | tf_op jit(solution)/shard_map/all_to_all | solution.py:558
  59.8 2.0 shard_map.215
  61.8 3.6 %collective-permute-start.3 = (f32[24,3072]{1,0:T(8,128)}, f32[24,3072]{1,0:T(8,128)S(1)}, u32[]{:S(2)}, u32[]{:S(2)}) collective-permute-start(f32[24,3072]{1,0:T(8,128)} %get-tuple-element.64.mine), channel_id=1, source_target_pairs={{0,32},{32,0},{1,33},{33,1},{2,34},{34,2},{3,35},{35,3},{4,36},{36... | collective-permute-start | bytes 884744 | tf_op jit(solution)/shard_map/ppermute | solution.py:562
  65.4 0.9 collective-permute-start.6
  66.3 2.0 collective-permute-start.5
  68.3 0.8 collective-permute-start.4
  69.1 0.0 collective-permute-done.3.other
  69.1 1.0 copy-done
  70.0 2.4 shard_map.216
  72.4 0.0 collective-permute-done.6.roots_three
  72.4 0.0 collective-permute-done.5.roots_two
  72.4 0.6 copy-done.5
  73.0 0.0 copy-done.6
  73.0 0.0 copy-done.7
  73.1 5.4 %all-to-all-start.2 = ((f32[64,8,1024]{2,1,0:T(8,128)}), f32[64,8,1024]{2,1,0:T(8,128)S(1)}, u32[]{:S(2)}, u32[]{:S(2)}) async-start(f32[64,8,1024]{2,1,0:T(8,128)} %bitcast.5), calls=%async_computation.2 | async-start | bytes 4194304 | tf_op jit(solution)/shard_map/all_to_all | solution.py:565
  78.5 39.7 %shard_map.217 = (f32[16,512]{1,0:T(8,128)}, f32[64,88,128]{2,1,0:T(8,128)}, f32[64,88,128]{2,1,0:T(8,128)}) custom-call(s32[1]{0:T(128)} %bitcast.group, f32[4,16,128]{2,1,0:T(8,128)} %get-tuple-element.63.d_roots, f32[4,16,128]{2,1,0:T(8,128)} %copy-done.7, f32[4,16,128]{2,1,0:T(8,128)} %copy-done.6, f32[4,16,128]{2,1,0:T(8,128)} %copy-done.5, ...), custom_call_target="tpu_custom_call" | custom-call | flops 12000000000 | bytes 20000000 | tf_op jit(solution)/shard_map/pallas_call | solution.py:507
  118.1 1.3 collective-permute-start.7
  119.4 0.1 reduce_sum.18
  119.6 1.6 broadcast_in_dim.4
  121.1 10.3 %all-to-all-start.3 = ((f32[64,8,1024]{2,1,0:T(8,128)}), f32[64,8,1024]{2,1,0:T(8,128)}, u32[]{:S(2)}, u32[]{:S(2)}) async-start(f32[64,8,1024]{2,1,0:T(8,128)} %broadcast_in_dim.4), calls=%async_computation.3 | async-start | bytes 4194304 | tf_op jit(solution)/shard_map/all_to_all | solution.py:526
  131.5 3.0 %add.12 = f32[64,88,128]{2,1,0:T(8,128)S(1)} add(f32[64,88,128]{2,1,0:T(8,128)} %get-tuple-element.81, f32[64,88,128]{2,1,0:T(8,128)} %collective-permute-done.7) | non-fusion elementwise | flops 720896 | bytes 8650752 | tf_op jit(solution)/shard_map/add | solution.py:579
  134.4 26.5 %all-to-all-done.3 = f32[64,8,1024]{2,1,0:T(8,128)} async-done(((f32[64,8,1024]{2,1,0:T(8,128)}), f32[64,8,1024]{2,1,0:T(8,128)}, u32[]{:S(2)}, u32[]{:S(2)}) %all-to-all-start.3) | async-done | bytes 2097184 | tf_op jit(solution)/shard_map/all_to_all | solution.py:526
  161.0 42.9 %all_to_all.31 = f32[64,88,128]{2,1,0:T(8,128)} all-to-all(f32[64,88,128]{2,1,0:T(8,128)S(1)} %add.12), channel_id=1, replica_groups=mesh['zh'=2,'co'=2,'zl'=2,'y'=4,'x'=4] {'zh','zl','y','x'}, dimensions={0} | all-to-all | bytes 5767168 | tf_op jit(solution)/shard_map/all_to_all | solution.py:580
  203.9 2.0 reduce_sum.19
  205.9 1.8 broadcast_in_dim.5
  207.6 6.4 %all-to-all-start.5 = ((f32[64,88,128]{2,1,0:T(8,128)}), f32[64,88,128]{2,1,0:T(8,128)S(1)}, u32[]{:S(2)}, u32[]{:S(2)}) async-start(f32[64,88,128]{2,1,0:T(8,128)} %broadcast_in_dim.5), calls=%async_computation.5 | async-start | bytes 5767168 | tf_op jit(solution)/shard_map/all_to_all | solution.py:526
  214.0 1.2 collective-permute-start.8
  215.2 4.0 %collective-permute-done.8.other = f32[512,1024]{1,0:T(8,128)S(1)} collective-permute-done((f32[512,1024]{1,0:T(8,128)}, f32[512,1024]{1,0:T(8,128)S(1)}, u32[]{:S(2)}, u32[]{:S(2)}) %collective-permute-start.8) | collective-permute-done | bytes 2097184 | tf_op jit(solution)/shard_map/ppermute | solution.py:562
  219.2 1.3 copy-done.4
  220.5 4.5 %shard_map.218 = (f32[512,512]{1,0:T(8,128)}, f32[512,1024]{1,0:T(8,128)}, f32[512,512]{1,0:T(8,128)}) custom-call(s32[1]{0:T(128)} %bitcast.4.core, f32[512,1024]{1,0:T(8,128)} %bitcast.6.mine, f32[512,1024]{1,0:T(8,128)} %copy-done.4), custom_call_target="tpu_custom_call" | custom-call | tf_op jit(solution)/shard_map/pallas_call | solution.py:507
  225.1 25.5 %all-to-all-done.5.near.own = f32[64,88,128]{2,1,0:T(8,128)S(1)} async-done(((f32[64,88,128]{2,1,0:T(8,128)}), f32[64,88,128]{2,1,0:T(8,128)S(1)}, u32[]{:S(2)}, u32[]{:S(2)}) %all-to-all-start.5) | async-done | bytes 2883616 | tf_op jit(solution)/shard_map/all_to_all | solution.py:526
  250.6 3.2 %collective-permute-start.9 = (f32[64,88,128]{2,1,0:T(8,128)S(1)}, f32[64,88,128]{2,1,0:T(8,128)S(1)}, u32[]{:S(2)}, u32[]{:S(2)}) collective-permute-start(f32[64,88,128]{2,1,0:T(8,128)S(1)} %all-to-all-done.5.near.own), channel_id=1, source_target_pairs={{0,32},{32,0},{1,33},{33,1},{2,34},{34,2},{3,35},{35,3},{4,36},{36... | collective-permute-start | bytes 8650760 | tf_op jit(solution)/shard_map/ppermute | solution.py:562
  253.8 1.6 shard_map.219
  255.4 3.3 %collective-permute-done.9.near = f32[64,88,128]{2,1,0:T(8,128)S(1)} collective-permute-done((f32[64,88,128]{2,1,0:T(8,128)S(1)}, f32[64,88,128]{2,1,0:T(8,128)S(1)}, u32[]{:S(2)}, u32[]{:S(2)}) %collective-permute-start.9) | collective-permute-done | bytes 2883616 | tf_op jit(solution)/shard_map/ppermute | solution.py:562
  258.7 2.3 shard_map.220
  (12 shorter events, 0.0 us)
Async XLA Ops:
  15.9 6.7 %collective-permute-start.2 = (f32[24,128]{1,0:T(8,128)}, f32[24,128]{1,0:T(8,128)S(1)}, u32[]{:S(2)}, u32[]{:S(2)}) collective-permute-start(f32[24,128]{1,0:T(8,128)} %get-tuple-element.59.roots), channel_id=1, source_target_pairs={{0,96},{32,64},{64,32},{96,0},{1,97},{33,65},{65,33},{97,1},{2,98}... | collective-permute-start | bytes 36872 | tf_op jit(solution)/shard_map/ppermute | solution.py:521
  20.9 4.3 %collective-permute-start.1 = (f32[24,128]{1,0:T(8,128)}, f32[24,128]{1,0:T(8,128)S(1)}, u32[]{:S(2)}, u32[]{:S(2)}) collective-permute-start(f32[24,128]{1,0:T(8,128)} %get-tuple-element.59.roots), channel_id=1, source_target_pairs={{0,64},{32,96},{64,0},{96,32},{1,65},{33,97},{65,1},{97,33},{2,66}... | collective-permute-start | bytes 36872 | tf_op jit(solution)/shard_map/ppermute | solution.py:521
  20.9 4.3 %collective-permute-start = (f32[24,128]{1,0:T(8,128)}, f32[24,128]{1,0:T(8,128)S(1)}, u32[]{:S(2)}, u32[]{:S(2)}) collective-permute-start(f32[24,128]{1,0:T(8,128)} %get-tuple-element.59.roots), channel_id=1, source_target_pairs={{0,32},{32,0},{64,96},{96,64},{1,33},{33,1},{65,97},{97,65},{2,34}... | collective-permute-start | bytes 36872 | tf_op jit(solution)/shard_map/ppermute | solution.py:521
  25.2 0.9 copy-start.1
  26.1 0.7 copy-start.3
  27.6 0.6 copy-start.2
  28.3 16.1 %all-to-all-start = ((f32[32,24,128]{2,1,0:T(8,128)}), f32[32,24,128]{2,1,0:T(8,128)S(1)}, u32[]{:S(2)}, u32[]{:S(2)}) async-start(f32[32,24,128]{2,1,0:T(8,128)} %get-tuple-element.60), calls=%async_computation | async-start | bytes 786432 | tf_op jit(solution)/shard_map/all_to_all | solution.py:556
  61.8 7.3 %collective-permute-start.3 = (f32[24,3072]{1,0:T(8,128)}, f32[24,3072]{1,0:T(8,128)S(1)}, u32[]{:S(2)}, u32[]{:S(2)}) collective-permute-start(f32[24,3072]{1,0:T(8,128)} %get-tuple-element.64.mine), channel_id=1, source_target_pairs={{0,32},{32,0},{1,33},{33,1},{2,34},{34,2},{3,35},{35,3},{4,36},{36... | collective-permute-start | bytes 884744 | tf_op jit(solution)/shard_map/ppermute | solution.py:562
  65.4 7.0 %collective-permute-start.6 = (f32[4,16,128]{2,1,0:T(8,128)}, f32[4,16,128]{2,1,0:T(8,128)S(1)}, u32[]{:S(2)}, u32[]{:S(2)}) collective-permute-start(f32[4,16,128]{2,1,0:T(8,128)} %get-tuple-element.63.d_roots), channel_id=1, source_target_pairs={{0,96},{32,64},{64,32},{96,0},{1,97},{33,65},{65,33},{97,1},{2,98}... | collective-permute-start | bytes 98312 | tf_op jit(solution)/shard_map/ppermute | solution.py:521
  66.3 6.1 %collective-permute-start.5 = (f32[4,16,128]{2,1,0:T(8,128)}, f32[4,16,128]{2,1,0:T(8,128)S(1)}, u32[]{:S(2)}, u32[]{:S(2)}) collective-permute-start(f32[4,16,128]{2,1,0:T(8,128)} %get-tuple-element.63.d_roots), channel_id=1, source_target_pairs={{0,64},{32,96},{64,0},{96,32},{1,65},{33,97},{65,1},{97,33},{2,66}... | collective-permute-start | bytes 98312 | tf_op jit(solution)/shard_map/ppermute | solution.py:521
  68.3 4.1 %collective-permute-start.4 = (f32[4,16,128]{2,1,0:T(8,128)}, f32[4,16,128]{2,1,0:T(8,128)S(1)}, u32[]{:S(2)}, u32[]{:S(2)}) collective-permute-start(f32[4,16,128]{2,1,0:T(8,128)} %get-tuple-element.63.d_roots), channel_id=1, source_target_pairs={{0,32},{32,0},{64,96},{96,64},{1,33},{33,1},{65,97},{97,65},{2,34}... | collective-permute-start | bytes 98312 | tf_op jit(solution)/shard_map/ppermute | solution.py:521
  69.1 1.0 copy-start
  72.4 0.6 copy-start.5
  72.4 0.6 copy-start.6
  72.4 0.6 copy-start.7
  73.1 45.1 %all-to-all-start.2 = ((f32[64,8,1024]{2,1,0:T(8,128)}), f32[64,8,1024]{2,1,0:T(8,128)S(1)}, u32[]{:S(2)}, u32[]{:S(2)}) async-start(f32[64,8,1024]{2,1,0:T(8,128)} %bitcast.5), calls=%async_computation.2 | async-start | bytes 4194304 | tf_op jit(solution)/shard_map/all_to_all | solution.py:565
  118.1 13.3 %collective-permute-start.7 = (f32[64,88,128]{2,1,0:T(8,128)}, f32[64,88,128]{2,1,0:T(8,128)}, u32[]{:S(2)}, u32[]{:S(2)}) collective-permute-start(f32[64,88,128]{2,1,0:T(8,128)} %get-tuple-element.84), channel_id=1, source_target_pairs={{0,32},{32,0},{1,33},{33,1},{2,34},{34,2},{3,35},{35,3},{4,36},{36... | collective-permute-start | bytes 8650760 | tf_op jit(solution)/shard_map/ppermute | solution.py:562
  121.1 39.8 %all-to-all-start.3 = ((f32[64,8,1024]{2,1,0:T(8,128)}), f32[64,8,1024]{2,1,0:T(8,128)}, u32[]{:S(2)}, u32[]{:S(2)}) async-start(f32[64,8,1024]{2,1,0:T(8,128)} %broadcast_in_dim.4), calls=%async_computation.3 | async-start | bytes 4194304 | tf_op jit(solution)/shard_map/all_to_all | solution.py:526
  207.6 43.0 %all-to-all-start.5 = ((f32[64,88,128]{2,1,0:T(8,128)}), f32[64,88,128]{2,1,0:T(8,128)S(1)}, u32[]{:S(2)}, u32[]{:S(2)}) async-start(f32[64,88,128]{2,1,0:T(8,128)} %broadcast_in_dim.5), calls=%async_computation.5 | async-start | bytes 5767168 | tf_op jit(solution)/shard_map/all_to_all | solution.py:526
  214.0 5.2 %collective-permute-start.8 = (f32[512,1024]{1,0:T(8,128)}, f32[512,1024]{1,0:T(8,128)S(1)}, u32[]{:S(2)}, u32[]{:S(2)}) collective-permute-start(f32[512,1024]{1,0:T(8,128)} %bitcast.6.mine), channel_id=1, source_target_pairs={{0,32},{32,0},{1,33},{33,1},{2,34},{34,2},{3,35},{35,3},{4,36},{36... | collective-permute-start | bytes 6291464 | tf_op jit(solution)/shard_map/ppermute | solution.py:562
  219.2 1.3 copy-start.4
  250.6 8.1 %collective-permute-start.9 = (f32[64,88,128]{2,1,0:T(8,128)S(1)}, f32[64,88,128]{2,1,0:T(8,128)S(1)}, u32[]{:S(2)}, u32[]{:S(2)}) collective-permute-start(f32[64,88,128]{2,1,0:T(8,128)S(1)} %all-to-all-done.5.near.own), channel_id=1, source_target_pairs={{0,32},{32,0},{1,33},{33,1},{2,34},{34,2},{3,35},{35,3},{4,36},{36... | collective-permute-start | bytes 8650760 | tf_op jit(solution)/shard_map/ppermute | solution.py:562
where the time goes:
time: 265 us; the launch traced here: 261 us
  Pallas kernels  71.4 us (27%)
  waiting for transfers between devices  71.4 us (27%)
  blocking collectives  55.6 us (21%)
  starting transfers between devices  48.3 us (18%)
  local copies, waits for them, and re-layouts  8.46 us (3%)
  other arithmetic  5.1 us (2%)
    pallas_call x7, Pallas kernels, run(): pl.pallas_call(kernel, out_shape=shapes, in_specs=specs, out_specs=[pl.Bl...  67.4 us
    all_to_all x2, waiting for transfers between devices, spread(): return lax.all_to_all(wide, axes, 0, 0, tiled=True)  52 us
    all_to_all x1, blocking collectives, shards(): late = jnp.sum(lax.all_to_all(late, CHIPS, 0, 0, tiled=True), axis=0)  42.9 us
    all_to_all x2, starting transfers between devices, spread(): return lax.all_to_all(wide, axes, 0, 0, tiled=True)  16.7 us
    all_to_all x1, blocking collectives, shards(): got = lax.all_to_all(message, LEAF, 0, 0, tiled=True)  12.6 us
    ppermute x4, starting transfers between devices, shards(): swap = lambda v: lax.ppermute(v, 'co', [(0, 1), (1, 0)])  9.28 us
    ppermute x6, starting transfers between devices, group_swaps(): lax.ppermute(value, GRP, [(i, i ^ k) for i in range(4)])  9.19 us
    all_to_all x1, waiting for transfers between devices, shards(): got = lax.all_to_all(message, LEAF, 0, 0, tiled=True)  8.29 us
  transfers between devices with their start and end apart: 14, of which 7 were waited for; matrix products, arithmetic and copies ran while one was open for 2% of the time, Pallas kernels for 18%

commit v1 on v0

--- a/solution.py
+++ b/solution.py
@@ -268,16 +268,24 @@
     )
     half = lambda at, width: both(pl.multiple_of(at + core[0] * width, 128), width)
     normed = both(2048, 512)
-    grads[:, :256] = t_mm(both(0, 512), half(2560, 256))
-    grads[:, 256:512] = t_mm(normed, half(512, 256))
-    grads[:, 512:] = t_mm(normed, half(1024, 512))
+    parts = (
+        t_mm(both(0, 512), half(2560, 256)),
+        t_mm(normed, half(512, 256)),
+        t_mm(normed, half(1024, 512)),
+    )
+    whole = jnp.concatenate(parts, axis=1)
+    for j in range(8):
+        block = whole[:, 128 * j : 128 * j + 128].reshape(64, 8, 128)
+        grads[:, 8 * j : 8 * j + 8, :] = block
 
 
 def assemble_upper_kernel(core, mine, other, grad_query, grad_keyval, grad_out):
     def fill(half, source):
-        grad_out[:, 256 * half : 256 * half + 256] = source[:, :256]
-        grad_query[:, 256 * half : 256 * half + 256] = source[:, 256:512]
-        grad_keyval[:, 512 * half : 512 * half + 512] = source[:, 512:]
+        homes = ((grad_out, 256, 0), (grad_query, 256, 2), (grad_keyval, 512, 4))
+        for home, width, first in homes:
+            for j in range(width // 128):
+                at, rows = width * half + 128 * j, 8 * (first + j)
+                home[:, at : at + 128] = source[:, rows : rows + 8, :].reshape(512, 128)
 
     for half in range(2):
 
@@ -401,6 +409,11 @@
     put(1, (32, 32), (80, 8), jnp.zeros((32, 8, 128), F32))
 
 
+def merge_kernel(upper, keep, other, both):
+    both[:, :64, :] = jnp.broadcast_to(upper[...].reshape(1, 64, 128), (64, 64, 128))
+    both[:, 64:, :] = keep[...] + other[...]
+
+
 def place(half, near, outs, staged, left):
     three, two, one = staged
     homes = (
@@ -560,9 +573,9 @@
         unpack_kernel, [(16, 512), (16, 512), (16, 1024), (4, 16, 128), (24, 3072)]
     )(got, rows, root_rows, cotangent)
     swap = lambda v: lax.ppermute(v, "co", [(0, 1), (1, 0)])
-    upper = call(upper_kernel, [(512, 1024)], (), True, limit=16)(core, pack, swap(pack))[0]
+    upper = call(upper_kernel, [(64, 64, 128)], (), True, limit=16)(core, pack, swap(pack))[0]
     upper, *far = lax.optimization_barrier((upper, *group_swaps(d_roots)))
-    upper = lax.all_to_all(upper.reshape(64, 8, 1024), CHIPS, 0, 0, tiled=True)
+    upper = lax.all_to_all(upper, CHIPS, 0, 0, tiled=True)
     output, keep, send = call(
         backward_kernel,
         [(16, 512), (64, 88, 128), (64, 88, 128)],
@@ -575,9 +588,11 @@
         *saved,
     )
     send, upper = lax.optimization_barrier((send, upper))
-    upper = spread(jnp.sum(upper, axis=0), CHIPS, 64).reshape(512, 1024)
-    late, upper = lax.optimization_barrier((keep + swap(send), upper))
-    late = jnp.sum(lax.all_to_all(late, CHIPS, 0, 0, tiled=True), axis=0)
+    both = call(merge_kernel, [(64, 152, 128)], limit=24)(
+        jnp.sum(upper, axis=0), keep, swap(send)
+    )[0]
+    both = lax.all_to_all(both, CHIPS, 0, 0, tiled=True)
+    upper, late = both[:, :64], jnp.sum(both[:, 64:], axis=0)
     late = spread(late, CHIPS, 64)
     upper = call(assemble_upper_kernel, [(512, 512), (512, 1024), (512, 512)], (), True)(
         core, upper, swap(upper)

time: 265 us -> 259 us (0.977)
  blocking collectives: 55.6 us -> 82.7 us
  waiting for transfers between devices: 71.4 us -> 47 us
  starting transfers between devices: 48.3 us -> 37.8 us
  local copies, waits for them, and re-layouts: 8.46 us -> 13.4 us
  other arithmetic: 5.1 us -> 1.9 us
    all_to_all x2 -> x1, waiting for transfers between devices: 52 us -> 24.5 us  [spread(): return lax.all_to_all(wide, axes, 0, 0, tiled=True)]
    all_to_all x1, blocking collectives: 42.9 us -> 70 us  [shards(): both = lax.all_to_all(both, CHIPS, 0, 0, tiled=True)]
    all_to_all x2 -> x1, starting transfers between devices: 16.7 us -> 6.85 us  [spread(): return lax.all_to_all(wide, axes, 0, 0, tiled=True)]
    unnamed x16 -> x24, local copies, waits for them, and re-layouts: 5.12 us -> 9.84 us
    ppermute x4, waiting for transfers between devices: 7.28 us -> 10.5 us  [shards(): swap = lambda v: lax.ppermute(v, 'co', [(0, 1), (1, 0)])]
    add x1 -> x0, other arithmetic: 2.98 us -> none  [shards(): late, upper = lax.optimization_barrier((keep + swap(send), upper))]
    pallas_call x7 -> x8, Pallas kernels: 67.4 us -> 67.6 us  [run(): pl.pallas_call(kernel, out_shape=shapes, in_specs=specs, out_specs=[pl.Bl...]
  transfers between devices with their start and end apart: 14 -> 13, of which waited for: 7 -> 7; matrix products, arithmetic and copies ran while one was open for 2% -> 1% of each run, Pallas kernels for 18% -> 19%
where the time goes in v1:
time: 259 us; the launch traced here: 255 us
  blocking collectives  82.7 us (32%)
  Pallas kernels  71.5 us (28%)
  waiting for transfers between devices  47 us (18%)
  starting transfers between devices  37.8 us (15%)
  local copies, waits for them, and re-layouts  13.4 us (5%)
    all_to_all x1, blocking collectives, shards(): both = lax.all_to_all(both, CHIPS, 0, 0, tiled=True)  70 us
    pallas_call x8, Pallas kernels, run(): pl.pallas_call(kernel, out_shape=shapes, in_specs=specs, out_specs=[pl.Bl...  67.6 us
    all_to_all x1, waiting for transfers between devices, spread(): return lax.all_to_all(wide, axes, 0, 0, tiled=True)  24.5 us
    all_to_all x1, blocking collectives, shards(): got = lax.all_to_all(message, LEAF, 0, 0, tiled=True)  12.6 us
    ppermute x4, waiting for transfers between devices, shards(): swap = lambda v: lax.ppermute(v, 'co', [(0, 1), (1, 0)])  10.5 us
    unnamed x24, local copies, waits for them, and re-layouts  9.84 us
    ppermute x6, starting transfers between devices, group_swaps(): lax.ppermute(value, GRP, [(i, i ^ k) for i in range(4)])  9.19 us
    ppermute x4, starting transfers between devices, shards(): swap = lambda v: lax.ppermute(v, 'co', [(0, 1), (1, 0)])  8.55 us
  transfers between devices with their start and end apart: 13, of which 7 were waited for; matrix products, arithmetic and copies ran while one was open for 1% of the time, Pallas kernels for 19%

profile of v1, /device:TPU:1, one launch (start us, length us, event | category | flops | bytes accessed | tf_op | source)
XLA Modules:
  0.0 255.3 jit_solution(3225531154113251249)
XLA Ops:
  0.6 15.2 %shard_map.212 = (f32[1024,128]{1,0:T(8,128)}, f32[1024,384]{1,0:T(8,128)}, f32[4096,128]{1,0:T(8,128)}, f32[1024,128]{1,0:T(8,128)}, f32[1024,128]{1,0:T(8,128)...) custom-call(s32[1,1024]{1,0:T(1,128)} %order.1, ...), custom_call_target="tpu_custom_call" | custom-call | tf_op jit(solution)/shard_map/pallas_call | solution.py:520
  15.9 5.1 %collective-permute-start.2 = (f32[24,128]{1,0:T(8,128)}, f32[24,128]{1,0:T(8,128)S(1)}, u32[]{:S(2)}, u32[]{:S(2)}) collective-permute-start(f32[24,128]{1,0:T(8,128)} %get-tuple-element.57.roots), channel_id=1, source_target_pairs={{0,96},{32,64},{64,32},{96,0},{1,97},{33,65},{65,33},{97,1},{2,98}... | collective-permute-start | bytes 36872 | tf_op jit(solution)/shard_map/ppermute | solution.py:534
  20.9 0.0 collective-permute-start.1
  20.9 0.5 collective-permute-start
  21.4 1.1 collective-permute-done.2.three
  22.5 2.7 %collective-permute-done.1.two = f32[24,128]{1,0:T(8,128)S(1)} collective-permute-done((f32[24,128]{1,0:T(8,128)}, f32[24,128]{1,0:T(8,128)S(1)}, u32[]{:S(2)}, u32[]{:S(2)}) %collective-permute-start.1) | collective-permute-done | bytes 12320 | tf_op jit(solution)/shard_map/ppermute | solution.py:534
  25.2 0.9 copy-done.2
  26.1 0.7 copy-done.4
  26.8 0.9 shard_map.213
  27.7 0.6 copy-done.3
  28.3 7.8 %all-to-all-start = ((f32[32,24,128]{2,1,0:T(8,128)}), f32[32,24,128]{2,1,0:T(8,128)S(1)}, u32[]{:S(2)}, u32[]{:S(2)}) async-start(f32[32,24,128]{2,1,0:T(8,128)} %get-tuple-element.58), calls=%async_computation | async-start | bytes 786432 | tf_op jit(solution)/shard_map/all_to_all | solution.py:569
  36.0 8.3 %all-to-all-done.got = f32[32,24,128]{2,1,0:T(8,128)S(1)} async-done(((f32[32,24,128]{2,1,0:T(8,128)}), f32[32,24,128]{2,1,0:T(8,128)S(1)}, u32[]{:S(2)}, u32[]{:S(2)}) %all-to-all-start) | async-done | bytes 393248 | tf_op jit(solution)/shard_map/all_to_all | solution.py:569
  44.3 2.9 %shard_map.214 = f32[32,24,128]{2,1,0:T(8,128)S(1)} custom-call(s32[1]{0:T(128)} %bitcast.1.half, f32[32,24,128]{2,1,0:T(8,128)S(1)} %all-to-all-done.got), custom_call_target="tpu_custom_call" | custom-call | tf_op jit(solution)/shard_map/pallas_call | solution.py:520
  47.2 12.6 %all_to_all.25.got = f32[32,24,128]{2,1,0:T(8,128)} all-to-all(f32[32,24,128]{2,1,0:T(8,128)S(1)} %shard_map.214), channel_id=1, replica_groups=mesh['zh'=2,'co'=2,'zl'=2,'y'=4,'x'=4] {'zl','y','x'}, dimensions={0} | all-to-all | bytes 786432 | tf_op jit(solution)/shard_map/all_to_all | solution.py:571
  59.8 2.0 shard_map.215
  61.8 3.6 %collective-permute-start.3 = (f32[24,3072]{1,0:T(8,128)}, f32[24,3072]{1,0:T(8,128)S(1)}, u32[]{:S(2)}, u32[]{:S(2)}) collective-permute-start(f32[24,3072]{1,0:T(8,128)} %get-tuple-element.62.mine), channel_id=1, source_target_pairs={{0,32},{32,0},{1,33},{33,1},{2,34},{34,2},{3,35},{35,3},{4,36},{36... | collective-permute-start | bytes 884744 | tf_op jit(solution)/shard_map/ppermute | solution.py:575
  65.4 0.9 collective-permute-start.6
  66.3 2.0 collective-permute-start.5
  68.3 0.8 collective-permute-start.4
  69.1 0.0 collective-permute-done.3.other
  69.1 1.0 copy-done.1
  70.0 2.4 shard_map.216
  72.4 0.0 collective-permute-done.4.roots_one
  72.5 5.4 %all-to-all-start.2 = ((f32[64,64,128]{2,1,0:T(8,128)}), f32[64,64,128]{2,1,0:T(8,128)S(1)}, u32[]{:S(2)}, u32[]{:S(2)}) async-start(f32[64,64,128]{2,1,0:T(8,128)} %shard_map.216), calls=%async_computation.2 | async-start | bytes 4194304 | tf_op jit(solution)/shard_map/all_to_all | solution.py:578
  77.9 39.3 %shard_map.217 = (f32[16,512]{1,0:T(8,128)}, f32[64,88,128]{2,1,0:T(8,128)}, f32[64,88,128]{2,1,0:T(8,128)}) custom-call(s32[1]{0:T(128)} %bitcast.group, f32[4,16,128]{2,1,0:T(8,128)} %get-tuple-element.61.d_roots, f32[4,16,128]{2,1,0:T(8,128)} %copy-done.11, f32[4,16,128]{2,1,0:T(8,128)} %copy-done.10, f32[4,16,128]{2,1,0:T(8,128)} %copy-done.9, ...), custom_call_target="tpu_custom_call" | custom-call | flops 12000000000 | bytes 20000000 | tf_op jit(solution)/shard_map/pallas_call | solution.py:520
  117.2 0.0 all-to-all-done.2
  117.2 0.0 copy-start.6
  117.2 1.3 copy-done.6
  118.5 1.2 collective-permute-start.7
  119.7 1.7 reduce_sum.18.upper
  121.4 3.4 %collective-permute-done.7.other = f32[64,88,128]{2,1,0:T(8,128)S(1)} collective-permute-done((f32[64,88,128]{2,1,0:T(8,128)}, f32[64,88,128]{2,1,0:T(8,128)S(1)}, u32[]{:S(2)}, u32[]{:S(2)}) %collective-permute-start.7) | collective-permute-done | bytes 2883616 | tf_op jit(solution)/shard_map/ppermute | solution.py:575
  124.8 1.8 copy-done
  126.6 0.4 shard_map.218
  127.1 70.0 %all_to_all.26 = f32[64,152,128]{2,1,0:T(8,128)S(1)} all-to-all(f32[64,152,128]{2,1,0:T(8,128)S(1)} %shard_map.218), channel_id=1, replica_groups=mesh['zh'=2,'co'=2,'zl'=2,'y'=4,'x'=4] {'zh','zl','y','x'}, dimensions={0} | all-to-all | bytes 9961472 | tf_op jit(solution)/shard_map/all_to_all | solution.py:594
  197.1 2.2 copy-done.5
  199.3 0.2 slice_reduce_fusion
  199.5 1.8 broadcast_in_dim.2
  201.2 6.8 %all-to-all-start.4 = ((f32[64,88,128]{2,1,0:T(8,128)}), f32[64,88,128]{2,1,0:T(8,128)S(1)}, u32[]{:S(2)}, u32[]{:S(2)}) async-start(f32[64,88,128]{2,1,0:T(8,128)} %broadcast_in_dim.2), calls=%async_computation.4 | async-start | bytes 5767168 | tf_op jit(solution)/shard_map/all_to_all | solution.py:539
  208.1 1.8 slice.9.mine
  209.9 0.9 collective-permute-start.8
  210.8 3.8 %collective-permute-done.8.other = f32[64,64,128]{2,1,0:T(8,128)S(1)} collective-permute-done((f32[64,64,128]{2,1,0:T(8,128)S(1)}, f32[64,64,128]{2,1,0:T(8,128)S(1)}, u32[]{:S(2)}, u32[]{:S(2)}) %collective-permute-start.8) | collective-permute-done | bytes 2097184 | tf_op jit(solution)/shard_map/ppermute | solution.py:575
  214.6 1.3 copy-done.8
  215.9 4.6 %shard_map.219 = (f32[512,512]{1,0:T(8,128)}, f32[512,1024]{1,0:T(8,128)}, f32[512,512]{1,0:T(8,128)}) custom-call(s32[1]{0:T(128)} %bitcast.4.core, f32[64,64,128]{2,1,0:T(8,128)} %copy-done.7, f32[64,64,128]{2,1,0:T(8,128)} %copy-done.8), custom_call_target="tpu_custom_call" | custom-call | tf_op jit(solution)/shard_map/pallas_call | solution.py:520
  220.5 24.5 %all-to-all-done.4.near.own = f32[64,88,128]{2,1,0:T(8,128)S(1)} async-done(((f32[64,88,128]{2,1,0:T(8,128)}), f32[64,88,128]{2,1,0:T(8,128)S(1)}, u32[]{:S(2)}, u32[]{:S(2)}) %all-to-all-start.4) | async-done | bytes 2883616 | tf_op jit(solution)/shard_map/all_to_all | solution.py:539
  245.0 2.9 %collective-permute-start.9 = (f32[64,88,128]{2,1,0:T(8,128)S(1)}, f32[64,88,128]{2,1,0:T(8,128)S(1)}, u32[]{:S(2)}, u32[]{:S(2)}) collective-permute-start(f32[64,88,128]{2,1,0:T(8,128)S(1)} %all-to-all-done.4.near.own), channel_id=1, source_target_pairs={{0,32},{32,0},{1,33},{33,1},{2,34},{34,2},{3,35},{35,3},{4,36},{36... | collective-permute-start | bytes 8650760 | tf_op jit(solution)/shard_map/ppermute | solution.py:575
  247.9 1.6 shard_map.220
  249.5 3.3 %collective-permute-done.9.near = f32[64,88,128]{2,1,0:T(8,128)S(1)} collective-permute-done((f32[64,88,128]{2,1,0:T(8,128)S(1)}, f32[64,88,128]{2,1,0:T(8,128)S(1)}, u32[]{:S(2)}, u32[]{:S(2)}) %collective-permute-start.9) | collective-permute-done | bytes 2883616 | tf_op jit(solution)/shard_map/ppermute | solution.py:575
  252.8 2.3 shard_map.221
  (18 shorter events, 0.0 us)
Async XLA Ops:
  15.9 6.7 %collective-permute-start.2 = (f32[24,128]{1,0:T(8,128)}, f32[24,128]{1,0:T(8,128)S(1)}, u32[]{:S(2)}, u32[]{:S(2)}) collective-permute-start(f32[24,128]{1,0:T(8,128)} %get-tuple-element.57.roots), channel_id=1, source_target_pairs={{0,96},{32,64},{64,32},{96,0},{1,97},{33,65},{65,33},{97,1},{2,98}... | collective-permute-start | bytes 36872 | tf_op jit(solution)/shard_map/ppermute | solution.py:534
  20.9 4.3 %collective-permute-start.1 = (f32[24,128]{1,0:T(8,128)}, f32[24,128]{1,0:T(8,128)S(1)}, u32[]{:S(2)}, u32[]{:S(2)}) collective-permute-start(f32[24,128]{1,0:T(8,128)} %get-tuple-element.57.roots), channel_id=1, source_target_pairs={{0,64},{32,96},{64,0},{96,32},{1,65},{33,97},{65,1},{97,33},{2,66}... | collective-permute-start | bytes 36872 | tf_op jit(solution)/shard_map/ppermute | solution.py:534
  20.9 4.3 %collective-permute-start = (f32[24,128]{1,0:T(8,128)}, f32[24,128]{1,0:T(8,128)S(1)}, u32[]{:S(2)}, u32[]{:S(2)}) collective-permute-start(f32[24,128]{1,0:T(8,128)} %get-tuple-element.57.roots), channel_id=1, source_target_pairs={{0,32},{32,0},{64,96},{96,64},{1,33},{33,1},{65,97},{97,65},{2,34}... | collective-permute-start | bytes 36872 | tf_op jit(solution)/shard_map/ppermute | solution.py:534
  25.2 0.9 copy-start.2
  26.1 0.7 copy-start.4
  27.6 0.6 copy-start.3
  28.3 16.1 %all-to-all-start = ((f32[32,24,128]{2,1,0:T(8,128)}), f32[32,24,128]{2,1,0:T(8,128)S(1)}, u32[]{:S(2)}, u32[]{:S(2)}) async-start(f32[32,24,128]{2,1,0:T(8,128)} %get-tuple-element.58), calls=%async_computation | async-start | bytes 786432 | tf_op jit(solution)/shard_map/all_to_all | solution.py:569
  61.8 7.3 %collective-permute-start.3 = (f32[24,3072]{1,0:T(8,128)}, f32[24,3072]{1,0:T(8,128)S(1)}, u32[]{:S(2)}, u32[]{:S(2)}) collective-permute-start(f32[24,3072]{1,0:T(8,128)} %get-tuple-element.62.mine), channel_id=1, source_target_pairs={{0,32},{32,0},{1,33},{33,1},{2,34},{34,2},{3,35},{35,3},{4,36},{36... | collective-permute-start | bytes 884744 | tf_op jit(solution)/shard_map/ppermute | solution.py:575
  65.4 7.0 %collective-permute-start.6 = (f32[4,16,128]{2,1,0:T(8,128)}, f32[4,16,128]{2,1,0:T(8,128)S(1)}, u32[]{:S(2)}, u32[]{:S(2)}) collective-permute-start(f32[4,16,128]{2,1,0:T(8,128)} %get-tuple-element.61.d_roots), channel_id=1, source_target_pairs={{0,96},{32,64},{64,32},{96,0},{1,97},{33,65},{65,33},{97,1},{2,98}... | collective-permute-start | bytes 98312 | tf_op jit(solution)/shard_map/ppermute | solution.py:534
  66.3 6.1 %collective-permute-start.5 = (f32[4,16,128]{2,1,0:T(8,128)}, f32[4,16,128]{2,1,0:T(8,128)S(1)}, u32[]{:S(2)}, u32[]{:S(2)}) collective-permute-start(f32[4,16,128]{2,1,0:T(8,128)} %get-tuple-element.61.d_roots), channel_id=1, source_target_pairs={{0,64},{32,96},{64,0},{96,32},{1,65},{33,97},{65,1},{97,33},{2,66}... | collective-permute-start | bytes 98312 | tf_op jit(solution)/shard_map/ppermute | solution.py:534
  68.3 4.2 %collective-permute-start.4 = (f32[4,16,128]{2,1,0:T(8,128)}, f32[4,16,128]{2,1,0:T(8,128)S(1)}, u32[]{:S(2)}, u32[]{:S(2)}) collective-permute-start(f32[4,16,128]{2,1,0:T(8,128)} %get-tuple-element.61.d_roots), channel_id=1, source_target_pairs={{0,32},{32,0},{64,96},{96,64},{1,33},{33,1},{65,97},{97,65},{2,34}... | collective-permute-start | bytes 98312 | tf_op jit(solution)/shard_map/ppermute | solution.py:534
  69.1 1.0 copy-start.1
  72.4 5.5 %copy-start.9 = (f32[4,16,128]{2,1,0:T(8,128)}, f32[4,16,128]{2,1,0:T(8,128)S(1)}, u32[]{:S(2)}) copy-start(f32[4,16,128]{2,1,0:T(8,128)S(1)} %collective-permute-done.6.roots_three) | copy-start | bytes 98308
  72.4 5.5 %copy-start.10 = (f32[4,16,128]{2,1,0:T(8,128)}, f32[4,16,128]{2,1,0:T(8,128)S(1)}, u32[]{:S(2)}) copy-start(f32[4,16,128]{2,1,0:T(8,128)S(1)} %collective-permute-done.5.roots_two) | copy-start | bytes 98308
  72.4 5.5 %copy-start.11 = (f32[4,16,128]{2,1,0:T(8,128)}, f32[4,16,128]{2,1,0:T(8,128)S(1)}, u32[]{:S(2)}) copy-start(f32[4,16,128]{2,1,0:T(8,128)S(1)} %collective-permute-done.4.roots_one) | copy-start | bytes 98308
  72.5 44.7 %all-to-all-start.2 = ((f32[64,64,128]{2,1,0:T(8,128)}), f32[64,64,128]{2,1,0:T(8,128)S(1)}, u32[]{:S(2)}, u32[]{:S(2)}) async-start(f32[64,64,128]{2,1,0:T(8,128)} %shard_map.216), calls=%async_computation.2 | async-start | bytes 4194304 | tf_op jit(solution)/shard_map/all_to_all | solution.py:578
  117.2 1.3 copy-start.6
  118.5 6.3 %collective-permute-start.7 = (f32[64,88,128]{2,1,0:T(8,128)}, f32[64,88,128]{2,1,0:T(8,128)S(1)}, u32[]{:S(2)}, u32[]{:S(2)}) collective-permute-start(f32[64,88,128]{2,1,0:T(8,128)} %get-tuple-element.83), channel_id=1, source_target_pairs={{0,32},{32,0},{1,33},{33,1},{2,34},{34,2},{3,35},{35,3},{4,36},{36... | collective-permute-start | bytes 8650760 | tf_op jit(solution)/shard_map/ppermute | solution.py:575
  124.8 1.8 copy-start
  197.1 2.2 copy-start.5
  201.2 43.7 %all-to-all-start.4 = ((f32[64,88,128]{2,1,0:T(8,128)}), f32[64,88,128]{2,1,0:T(8,128)S(1)}, u32[]{:S(2)}, u32[]{:S(2)}) async-start(f32[64,88,128]{2,1,0:T(8,128)} %broadcast_in_dim.2), calls=%async_computation.4 | async-start | bytes 5767168 | tf_op jit(solution)/shard_map/all_to_all | solution.py:539
  209.9 4.7 %copy-start.7 = (f32[64,64,128]{2,1,0:T(8,128)}, f32[64,64,128]{2,1,0:T(8,128)S(1)}, u32[]{:S(2)}) copy-start(f32[64,64,128]{2,1,0:T(8,128)S(1)} %slice.9.mine) | copy-start | bytes 6291460
  209.9 4.6 %collective-permute-start.8 = (f32[64,64,128]{2,1,0:T(8,128)S(1)}, f32[64,64,128]{2,1,0:T(8,128)S(1)}, u32[]{:S(2)}, u32[]{:S(2)}) collective-permute-start(f32[64,64,128]{2,1,0:T(8,128)S(1)} %slice.9.mine), channel_id=1, source_target_pairs={{0,32},{32,0},{1,33},{33,1},{2,34},{34,2},{3,35},{35,3},{4,36},{36... | collective-permute-start | bytes 6291464 | tf_op jit(solution)/shard_map/ppermute | solution.py:575
  214.6 1.3 copy-start.8
  245.0 7.8 %collective-permute-start.9 = (f32[64,88,128]{2,1,0:T(8,128)S(1)}, f32[64,88,128]{2,1,0:T(8,128)S(1)}, u32[]{:S(2)}, u32[]{:S(2)}) collective-permute-start(f32[64,88,128]{2,1,0:T(8,128)S(1)} %all-to-all-done.4.near.own), channel_id=1, source_target_pairs={{0,32},{32,0},{1,33},{33,1},{2,34},{34,2},{3,35},{35,3},{4,36},{36... | collective-permute-start | bytes 8650760 | tf_op jit(solution)/shard_map/ppermute | solution.py:575

commit v2 on v1

--- a/solution.py
+++ b/solution.py
@@ -414,6 +414,11 @@
     both[:, 64:, :] = keep[...] + other[...]
 
 
+def spread_kernel(both, wide):
+    total = jnp.sum(both[:, 64:, :], axis=0, keepdims=True)
+    wide[...] = jnp.broadcast_to(total, (64, 88, 128))
+
+
 def place(half, near, outs, staged, left):
     three, two, one = staged
     homes = (
@@ -532,11 +537,6 @@
 
 def group_swaps(value):
     return [lax.ppermute(value, GRP, [(i, i ^ k) for i in range(4)]) for k in range(1, 4)]
-
-
-def spread(value, axes, parts):
-    wide = jnp.broadcast_to(value[None], (parts,) + value.shape)
-    return lax.all_to_all(wide, axes, 0, 0, tiled=True)
 
 
 def shards(
@@ -592,8 +592,9 @@
         jnp.sum(upper, axis=0), keep, swap(send)
     )[0]
     both = lax.all_to_all(both, CHIPS, 0, 0, tiled=True)
-    upper, late = both[:, :64], jnp.sum(both[:, 64:], axis=0)
-    late = spread(late, CHIPS, 64)
+    late = call(spread_kernel, [(64, 88, 128)], limit=24)(both)[0]
+    late = lax.all_to_all(late, CHIPS, 0, 0, tiled=True)
+    upper = both[:, :64]
     upper = call(assemble_upper_kernel, [(512, 512), (512, 1024), (512, 512)], (), True)(
         core, upper, swap(upper)
     )

time: 259 us -> 259 us (level)
    unnamed x24 -> x26, local copies, waits for them, and re-layouts: 9.84 us -> 11.4 us
    pallas_call x8 -> x9, Pallas kernels: 67.6 us -> 67.8 us  [run(): pl.pallas_call(kernel, out_shape=shapes, in_specs=specs, out_specs=[pl.Bl...]
where the time goes in v2:
time: 259 us; the launch traced here: 255 us
  blocking collectives  82.7 us (32%)
  Pallas kernels  71.8 us (28%)
  waiting for transfers between devices  47 us (18%)
  starting transfers between devices  37.8 us (15%)
  local copies, waits for them, and re-layouts  13.3 us (5%)
    all_to_all x1, blocking collectives, shards(): both = lax.all_to_all(both, CHIPS, 0, 0, tiled=True)  70 us
    pallas_call x9, Pallas kernels, run(): pl.pallas_call(kernel, out_shape=shapes, in_specs=specs, out_specs=[pl.Bl...  67.8 us
    all_to_all x1, waiting for transfers between devices, shards(): late = lax.all_to_all(late, CHIPS, 0, 0, tiled=True)  24.5 us
    all_to_all x1, blocking collectives, shards(): got = lax.all_to_all(message, LEAF, 0, 0, tiled=True)  12.6 us
    unnamed x26, local copies, waits for them, and re-layouts  11.4 us
    ppermute x4, waiting for transfers between devices, shards(): swap = lambda v: lax.ppermute(v, 'co', [(0, 1), (1, 0)])  10.5 us
    ppermute x6, starting transfers between devices, group_swaps(): lax.ppermute(value, GRP, [(i, i ^ k) for i in range(4)])  9.19 us
    ppermute x4, starting transfers between devices, shards(): swap = lambda v: lax.ppermute(v, 'co', [(0, 1), (1, 0)])  8.54 us
  transfers between devices with their start and end apart: 13, of which 7 were waited for; matrix products, arithmetic and copies ran while one was open for 1% of the time, Pallas kernels for 19%

profile of v2, /device:TPU:1, one launch (start us, length us, event | category | flops | bytes accessed | tf_op | source)
XLA Modules:
  0.0 255.2 jit_solution(13174608396526893018)
XLA Ops:
  0.6 15.2 %shard_map.212 = (f32[1024,128]{1,0:T(8,128)}, f32[1024,384]{1,0:T(8,128)}, f32[4096,128]{1,0:T(8,128)}, f32[1024,128]{1,0:T(8,128)}, f32[1024,128]{1,0:T(8,128)...) custom-call(s32[1,1024]{1,0:T(1,128)} %order.1, ...), custom_call_target="tpu_custom_call" | custom-call | tf_op jit(solution)/shard_map/pallas_call | solution.py:525
  15.9 5.1 %collective-permute-start.2 = (f32[24,128]{1,0:T(8,128)}, f32[24,128]{1,0:T(8,128)S(1)}, u32[]{:S(2)}, u32[]{:S(2)}) collective-permute-start(f32[24,128]{1,0:T(8,128)} %get-tuple-element.57.roots), channel_id=1, source_target_pairs={{0,96},{32,64},{64,32},{96,0},{1,97},{33,65},{65,33},{97,1},{2,98}... | collective-permute-start | bytes 36872 | tf_op jit(solution)/shard_map/ppermute | solution.py:539
  20.9 0.0 collective-permute-start.1
  20.9 0.5 collective-permute-start
  21.4 1.1 collective-permute-done.2.three
  22.5 2.7 %collective-permute-done.1.two = f32[24,128]{1,0:T(8,128)S(1)} collective-permute-done((f32[24,128]{1,0:T(8,128)}, f32[24,128]{1,0:T(8,128)S(1)}, u32[]{:S(2)}, u32[]{:S(2)}) %collective-permute-start.1) | collective-permute-done | bytes 12320 | tf_op jit(solution)/shard_map/ppermute | solution.py:539
  25.2 0.9 copy-done.4
  26.1 0.7 copy-done.6
  26.8 0.9 shard_map.213
  27.7 0.6 copy-done.5
  28.3 7.8 %all-to-all-start = ((f32[32,24,128]{2,1,0:T(8,128)}), f32[32,24,128]{2,1,0:T(8,128)S(1)}, u32[]{:S(2)}, u32[]{:S(2)}) async-start(f32[32,24,128]{2,1,0:T(8,128)} %get-tuple-element.58), calls=%async_computation | async-start | bytes 786432 | tf_op jit(solution)/shard_map/all_to_all | solution.py:569
  36.0 8.3 %all-to-all-done.got = f32[32,24,128]{2,1,0:T(8,128)S(1)} async-done(((f32[32,24,128]{2,1,0:T(8,128)}), f32[32,24,128]{2,1,0:T(8,128)S(1)}, u32[]{:S(2)}, u32[]{:S(2)}) %all-to-all-start) | async-done | bytes 393248 | tf_op jit(solution)/shard_map/all_to_all | solution.py:569
  44.3 2.9 %shard_map.214 = f32[32,24,128]{2,1,0:T(8,128)S(1)} custom-call(s32[1]{0:T(128)} %bitcast.1.half, f32[32,24,128]{2,1,0:T(8,128)S(1)} %all-to-all-done.got), custom_call_target="tpu_custom_call" | custom-call | tf_op jit(solution)/shard_map/pallas_call | solution.py:525
  47.2 12.6 %all_to_all.25.got = f32[32,24,128]{2,1,0:T(8,128)} all-to-all(f32[32,24,128]{2,1,0:T(8,128)S(1)} %shard_map.214), channel_id=1, replica_groups=mesh['zh'=2,'co'=2,'zl'=2,'y'=4,'x'=4] {'zl','y','x'}, dimensions={0} | all-to-all | bytes 786432 | tf_op jit(solution)/shard_map/all_to_all | solution.py:571
  59.8 2.0 shard_map.215
  61.8 3.6 %collective-permute-start.3 = (f32[24,3072]{1,0:T(8,128)}, f32[24,3072]{1,0:T(8,128)S(1)}, u32[]{:S(2)}, u32[]{:S(2)}) collective-permute-start(f32[24,3072]{1,0:T(8,128)} %get-tuple-element.62.mine), channel_id=1, source_target_pairs={{0,32},{32,0},{1,33},{33,1},{2,34},{34,2},{3,35},{35,3},{4,36},{36... | collective-permute-start | bytes 884744 | tf_op jit(solution)/shard_map/ppermute | solution.py:575
  65.4 0.9 collective-permute-start.6
  66.3 2.0 collective-permute-start.5
  68.3 0.8 collective-permute-start.4
  69.1 0.0 collective-permute-done.3.other
  69.1 1.0 copy-done.3
  70.0 2.4 shard_map.216
  72.4 0.0 collective-permute-done.6.roots_three
  72.4 0.0 collective-permute-done.5.roots_two
  72.5 5.4 %all-to-all-start.2 = ((f32[64,64,128]{2,1,0:T(8,128)}), f32[64,64,128]{2,1,0:T(8,128)S(1)}, u32[]{:S(2)}, u32[]{:S(2)}) async-start(f32[64,64,128]{2,1,0:T(8,128)} %shard_map.216), calls=%async_computation.2 | async-start | bytes 4194304 | tf_op jit(solution)/shard_map/all_to_all | solution.py:578
  77.9 39.3 %shard_map.217 = (f32[16,512]{1,0:T(8,128)}, f32[64,88,128]{2,1,0:T(8,128)}, f32[64,88,128]{2,1,0:T(8,128)}) custom-call(s32[1]{0:T(128)} %bitcast.group, f32[4,16,128]{2,1,0:T(8,128)} %get-tuple-element.61.d_roots, f32[4,16,128]{2,1,0:T(8,128)} %copy-done.12, f32[4,16,128]{2,1,0:T(8,128)} %copy-done.11, f32[4,16,128]{2,1,0:T(8,128)} %copy-done.10, ...), custom_call_target="tpu_custom_call" | custom-call | flops 12000000000 | bytes 20000000 | tf_op jit(solution)/shard_map/pallas_call | solution.py:525
  117.2 0.0 copy-start.7
  117.2 1.3 copy-done.7
  118.5 1.2 collective-permute-start.7
  119.7 1.7 reduce_sum.9.upper
  121.4 3.4 %collective-permute-done.7.other = f32[64,88,128]{2,1,0:T(8,128)S(1)} collective-permute-done((f32[64,88,128]{2,1,0:T(8,128)}, f32[64,88,128]{2,1,0:T(8,128)S(1)}, u32[]{:S(2)}, u32[]{:S(2)}) %collective-permute-start.7) | collective-permute-done | bytes 2883616 | tf_op jit(solution)/shard_map/ppermute | solution.py:575
  124.8 1.8 copy-done.2
  126.6 0.4 shard_map.218
  127.0 70.0 %all_to_all.26.both = f32[64,152,128]{2,1,0:T(8,128)S(1)} all-to-all(f32[64,152,128]{2,1,0:T(8,128)S(1)} %shard_map.218), channel_id=1, replica_groups=mesh['zh'=2,'co'=2,'zl'=2,'y'=4,'x'=4] {'zh','zl','y','x'}, dimensions={0} | all-to-all | bytes 9961472 | tf_op jit(solution)/shard_map/all_to_all | solution.py:594
  197.1 0.3 shard_map.219
  197.3 2.2 copy-done
  199.6 1.6 copy-done.1
  201.1 6.8 %all-to-all-start.4 = ((f32[64,88,128]{2,1,0:T(8,128)}), f32[64,88,128]{2,1,0:T(8,128)S(1)}, u32[]{:S(2)}, u32[]{:S(2)}) async-start(f32[64,88,128]{2,1,0:T(8,128)} %copy-done.1), calls=%async_computation.4 | async-start | bytes 5767168 | tf_op jit(solution)/shard_map/all_to_all | solution.py:596
  208.0 1.8 slice.4.mine
  209.8 0.9 collective-permute-start.8
  210.7 3.8 %collective-permute-done.8.other = f32[64,64,128]{2,1,0:T(8,128)S(1)} collective-permute-done((f32[64,64,128]{2,1,0:T(8,128)S(1)}, f32[64,64,128]{2,1,0:T(8,128)S(1)}, u32[]{:S(2)}, u32[]{:S(2)}) %collective-permute-start.8) | collective-permute-done | bytes 2097184 | tf_op jit(solution)/shard_map/ppermute | solution.py:575
  214.5 1.3 copy-done.9
  215.8 4.6 %shard_map.220 = (f32[512,512]{1,0:T(8,128)}, f32[512,1024]{1,0:T(8,128)}, f32[512,512]{1,0:T(8,128)}) custom-call(s32[1]{0:T(128)} %bitcast.4.core, f32[64,64,128]{2,1,0:T(8,128)} %copy-done.8, f32[64,64,128]{2,1,0:T(8,128)} %copy-done.9), custom_call_target="tpu_custom_call" | custom-call | tf_op jit(solution)/shard_map/pallas_call | solution.py:525
  220.4 24.5 %all-to-all-done.4.near.own = f32[64,88,128]{2,1,0:T(8,128)S(1)} async-done(((f32[64,88,128]{2,1,0:T(8,128)}), f32[64,88,128]{2,1,0:T(8,128)S(1)}, u32[]{:S(2)}, u32[]{:S(2)}) %all-to-all-start.4) | async-done | bytes 2883616 | tf_op jit(solution)/shard_map/all_to_all | solution.py:596
  244.9 2.9 %collective-permute-start.9 = (f32[64,88,128]{2,1,0:T(8,128)S(1)}, f32[64,88,128]{2,1,0:T(8,128)S(1)}, u32[]{:S(2)}, u32[]{:S(2)}) collective-permute-start(f32[64,88,128]{2,1,0:T(8,128)S(1)} %all-to-all-done.4.near.own), channel_id=1, source_target_pairs={{0,32},{32,0},{1,33},{33,1},{2,34},{34,2},{3,35},{35,3},{4,36},{36... | collective-permute-start | bytes 8650760 | tf_op jit(solution)/shard_map/ppermute | solution.py:575
  247.8 1.6 shard_map.221
  249.4 3.3 %collective-permute-done.9.near = f32[64,88,128]{2,1,0:T(8,128)S(1)} collective-permute-done((f32[64,88,128]{2,1,0:T(8,128)S(1)}, f32[64,88,128]{2,1,0:T(8,128)S(1)}, u32[]{:S(2)}, u32[]{:S(2)}) %collective-permute-start.9) | collective-permute-done | bytes 2883616 | tf_op jit(solution)/shard_map/ppermute | solution.py:575
  252.7 2.3 shard_map.222
  (19 shorter events, 0.0 us)
Async XLA Ops:
  15.9 6.7 %collective-permute-start.2 = (f32[24,128]{1,0:T(8,128)}, f32[24,128]{1,0:T(8,128)S(1)}, u32[]{:S(2)}, u32[]{:S(2)}) collective-permute-start(f32[24,128]{1,0:T(8,128)} %get-tuple-element.57.roots), channel_id=1, source_target_pairs={{0,96},{32,64},{64,32},{96,0},{1,97},{33,65},{65,33},{97,1},{2,98}... | collective-permute-start | bytes 36872 | tf_op jit(solution)/shard_map/ppermute | solution.py:539
  20.9 4.3 %collective-permute-start.1 = (f32[24,128]{1,0:T(8,128)}, f32[24,128]{1,0:T(8,128)S(1)}, u32[]{:S(2)}, u32[]{:S(2)}) collective-permute-start(f32[24,128]{1,0:T(8,128)} %get-tuple-element.57.roots), channel_id=1, source_target_pairs={{0,64},{32,96},{64,0},{96,32},{1,65},{33,97},{65,1},{97,33},{2,66}... | collective-permute-start | bytes 36872 | tf_op jit(solution)/shard_map/ppermute | solution.py:539
  20.9 4.3 %collective-permute-start = (f32[24,128]{1,0:T(8,128)}, f32[24,128]{1,0:T(8,128)S(1)}, u32[]{:S(2)}, u32[]{:S(2)}) collective-permute-start(f32[24,128]{1,0:T(8,128)} %get-tuple-element.57.roots), channel_id=1, source_target_pairs={{0,32},{32,0},{64,96},{96,64},{1,33},{33,1},{65,97},{97,65},{2,34}... | collective-permute-start | bytes 36872 | tf_op jit(solution)/shard_map/ppermute | solution.py:539
  25.2 0.9 copy-start.4
  26.1 0.7 copy-start.6
  27.6 0.6 copy-start.5
  28.3 16.1 %all-to-all-start = ((f32[32,24,128]{2,1,0:T(8,128)}), f32[32,24,128]{2,1,0:T(8,128)S(1)}, u32[]{:S(2)}, u32[]{:S(2)}) async-start(f32[32,24,128]{2,1,0:T(8,128)} %get-tuple-element.58), calls=%async_computation | async-start | bytes 786432 | tf_op jit(solution)/shard_map/all_to_all | solution.py:569
  61.8 7.3 %collective-permute-start.3 = (f32[24,3072]{1,0:T(8,128)}, f32[24,3072]{1,0:T(8,128)S(1)}, u32[]{:S(2)}, u32[]{:S(2)}) collective-permute-start(f32[24,3072]{1,0:T(8,128)} %get-tuple-element.62.mine), channel_id=1, source_target_pairs={{0,32},{32,0},{1,33},{33,1},{2,34},{34,2},{3,35},{35,3},{4,36},{36... | collective-permute-start | bytes 884744 | tf_op jit(solution)/shard_map/ppermute | solution.py:575
  65.4 7.0 %collective-permute-start.6 = (f32[4,16,128]{2,1,0:T(8,128)}, f32[4,16,128]{2,1,0:T(8,128)S(1)}, u32[]{:S(2)}, u32[]{:S(2)}) collective-permute-start(f32[4,16,128]{2,1,0:T(8,128)} %get-tuple-element.61.d_roots), channel_id=1, source_target_pairs={{0,96},{32,64},{64,32},{96,0},{1,97},{33,65},{65,33},{97,1},{2,98}... | collective-permute-start | bytes 98312 | tf_op jit(solution)/shard_map/ppermute | solution.py:539
  66.3 6.1 %collective-permute-start.5 = (f32[4,16,128]{2,1,0:T(8,128)}, f32[4,16,128]{2,1,0:T(8,128)S(1)}, u32[]{:S(2)}, u32[]{:S(2)}) collective-permute-start(f32[4,16,128]{2,1,0:T(8,128)} %get-tuple-element.61.d_roots), channel_id=1, source_target_pairs={{0,64},{32,96},{64,0},{96,32},{1,65},{33,97},{65,1},{97,33},{2,66}... | collective-permute-start | bytes 98312 | tf_op jit(solution)/shard_map/ppermute | solution.py:539
  68.3 4.1 %collective-permute-start.4 = (f32[4,16,128]{2,1,0:T(8,128)}, f32[4,16,128]{2,1,0:T(8,128)S(1)}, u32[]{:S(2)}, u32[]{:S(2)}) collective-permute-start(f32[4,16,128]{2,1,0:T(8,128)} %get-tuple-element.61.d_roots), channel_id=1, source_target_pairs={{0,32},{32,0},{64,96},{96,64},{1,33},{33,1},{65,97},{97,65},{2,34}... | collective-permute-start | bytes 98312 | tf_op jit(solution)/shard_map/ppermute | solution.py:539
  69.1 1.0 copy-start.3
  72.4 5.5 %copy-start.10 = (f32[4,16,128]{2,1,0:T(8,128)}, f32[4,16,128]{2,1,0:T(8,128)S(1)}, u32[]{:S(2)}) copy-start(f32[4,16,128]{2,1,0:T(8,128)S(1)} %collective-permute-done.6.roots_three) | copy-start | bytes 98308
  72.4 5.5 %copy-start.11 = (f32[4,16,128]{2,1,0:T(8,128)}, f32[4,16,128]{2,1,0:T(8,128)S(1)}, u32[]{:S(2)}) copy-start(f32[4,16,128]{2,1,0:T(8,128)S(1)} %collective-permute-done.5.roots_two) | copy-start | bytes 98308
  72.4 5.5 %copy-start.12 = (f32[4,16,128]{2,1,0:T(8,128)}, f32[4,16,128]{2,1,0:T(8,128)S(1)}, u32[]{:S(2)}) copy-start(f32[4,16,128]{2,1,0:T(8,128)S(1)} %collective-permute-done.4.roots_one) | copy-start | bytes 98308
  72.5 44.8 %all-to-all-start.2 = ((f32[64,64,128]{2,1,0:T(8,128)}), f32[64,64,128]{2,1,0:T(8,128)S(1)}, u32[]{:S(2)}, u32[]{:S(2)}) async-start(f32[64,64,128]{2,1,0:T(8,128)} %shard_map.216), calls=%async_computation.2 | async-start | bytes 4194304 | tf_op jit(solution)/shard_map/all_to_all | solution.py:578
  117.2 1.3 copy-start.7
  118.5 6.3 %collective-permute-start.7 = (f32[64,88,128]{2,1,0:T(8,128)}, f32[64,88,128]{2,1,0:T(8,128)S(1)}, u32[]{:S(2)}, u32[]{:S(2)}) collective-permute-start(f32[64,88,128]{2,1,0:T(8,128)} %get-tuple-element.83), channel_id=1, source_target_pairs={{0,32},{32,0},{1,33},{33,1},{2,34},{34,2},{3,35},{35,3},{4,36},{36... | collective-permute-start | bytes 8650760 | tf_op jit(solution)/shard_map/ppermute | solution.py:575
  124.8 1.8 copy-start.2
  197.3 2.2 copy-start
  199.6 1.6 copy-start.1
  201.1 43.7 %all-to-all-start.4 = ((f32[64,88,128]{2,1,0:T(8,128)}), f32[64,88,128]{2,1,0:T(8,128)S(1)}, u32[]{:S(2)}, u32[]{:S(2)}) async-start(f32[64,88,128]{2,1,0:T(8,128)} %copy-done.1), calls=%async_computation.4 | async-start | bytes 5767168 | tf_op jit(solution)/shard_map/all_to_all | solution.py:596
  209.8 4.7 %copy-start.8 = (f32[64,64,128]{2,1,0:T(8,128)}, f32[64,64,128]{2,1,0:T(8,128)S(1)}, u32[]{:S(2)}) copy-start(f32[64,64,128]{2,1,0:T(8,128)S(1)} %slice.4.mine) | copy-start | bytes 6291460
  209.8 4.6 %collective-permute-start.8 = (f32[64,64,128]{2,1,0:T(8,128)S(1)}, f32[64,64,128]{2,1,0:T(8,128)S(1)}, u32[]{:S(2)}, u32[]{:S(2)}) collective-permute-start(f32[64,64,128]{2,1,0:T(8,128)S(1)} %slice.4.mine), channel_id=1, source_target_pairs={{0,32},{32,0},{1,33},{33,1},{2,34},{34,2},{3,35},{35,3},{4,36},{36... | collective-permute-start | bytes 6291464 | tf_op jit(solution)/shard_map/ppermute | solution.py:575
  214.5 1.3 copy-start.9
  244.9 7.8 %collective-permute-start.9 = (f32[64,88,128]{2,1,0:T(8,128)S(1)}, f32[64,88,128]{2,1,0:T(8,128)S(1)}, u32[]{:S(2)}, u32[]{:S(2)}) collective-permute-start(f32[64,88,128]{2,1,0:T(8,128)S(1)} %all-to-all-done.4.near.own), channel_id=1, source_target_pairs={{0,32},{32,0},{1,33},{33,1},{2,34},{34,2},{3,35},{35,3},{4,36},{36... | collective-permute-start | bytes 8650760 | tf_op jit(solution)/shard_map/ppermute | solution.py:575
